TPU v7x, 256 devices: a whole 4x4x8 slice. The times are simulated.
256 devices in a mesh: row: 16 (over x, z_lo, core), col: 16 (over y, z_hi).
Axes of the slice: x: 4, y: 4, z: 8 (z_hi: 4, z_lo: 2; z = z_hi * 2 + z_lo), core: 2. Of those that a mesh axis runs over, the one named last changes fastest.
Arguments:
- obj: float32 [2, 2, 4096, 4096], P(None, None, 'row', 'col'), may hold values from -1.5 to 1.5
- probe: float32 [2, 256, 256], replicated, may hold values from -5 to 5
- amplitude: float32 [16, 16, 2, 1, 256, 256], P('row', 'col'), may hold values from 0 to 2
- positions: int32 [16, 16, 2, 1, 2], P('row', 'col'), may hold values from 0 to 256
Outputs:
- updated: float32 [2, 2, 4096, 4096], P(None, None, 'row', 'col')
Inputs may be any that keep to these rules, and one draw needn't show every extreme that they name: `positions`: every probe window lies inside its tile's region widened by 128 pixels on each side.
All inputs are finite; a program needn't handle non-finite values.
Results may differ from a plain program's by a relative error of at most 0.0003.
Values sent between devices are 32-bit elements; how exact they have to be, the bound alone decides.
A program may use at most 64 MiB of HBM per device.

v0:
```python
import math

import jax
import jax.numpy as jnp
from jax import lax
from jax.sharding import PartitionSpec as P

TILE = 256
MARGIN = 128


step_size = 0.5
highest = lax.Precision.HIGHEST


def from_behind(value, axis, steps):
    count = lax.axis_size(axis)
    initial, last = (max(0, -steps), min(count, count - steps))
    return lax.ppermute(value, axis, [(source, source + steps) for source in range(initial, last)])


def padded(cells, sides, width):
    for axis, dim in sides:
        count = lax.axis_size(axis)
        ends = count - 1
        head = lax.slice_in_dim(cells, 0, width, axis=dim)
        tail = lax.slice_in_dim(cells, cells.shape[dim] - width, cells.shape[dim], axis=dim)
        cells = jnp.concatenate(
            [
                lax.ppermute(tail, axis, [(i, (i + 1) % count) for i in range(ends)]),
                cells,
                lax.ppermute(head, axis, [((i + 1) % count, i) for i in range(ends)]),
            ],
            axis=dim,
        )
    return cells


def tables(size):
    index = lax.iota(jnp.int32, size)
    product = index[:, None] * index[None, :] % size
    angle = 2.0 * math.pi / size * product.astype(jnp.float32)
    norm = 1.0 / math.sqrt(size)
    return (jnp.cos(angle) * norm, -jnp.sin(angle) * norm)


def fresnel(size):
    index = lax.iota(jnp.int32, size)
    freq = jnp.where(index < size // 2, index, index - size)
    square = (freq[:, None] * freq[:, None] + freq[None, :] * freq[None, :]) % (4 * size)
    phase = math.pi / (2 * size) * square.astype(jnp.float32)
    return (jnp.cos(phase), -jnp.sin(phase))


def cmul(left_re, left_im, right_re, right_im):
    return (left_re * right_re - left_im * right_im, left_re * right_im + left_im * right_re)


def transform(field, table_re, table_im):
    stacked = jnp.stack(field, 0)
    block = jnp.stack([jnp.stack([table_re, -table_im], 1), jnp.stack([table_im, table_re], 1)], 0)
    left = jnp.einsum("ckdj,dbjl->cbkl", block, stacked, precision=highest)
    right_block = jnp.stack(
        [jnp.stack([table_re, table_im], 1), jnp.stack([-table_im, table_re], 1)], 0
    )
    out = jnp.einsum("dbkj,djcl->cbkl", left, right_block, precision=highest)
    return (out[0], out[1])


def margin_sum(total):
    side = total.shape[2] - 2 * MARGIN
    from_east = from_behind(total[:, :, :, :MARGIN], "col", -1)
    from_west = from_behind(total[:, :, :, side + MARGIN :], "col", 1)
    middle = total[:, :, :, MARGIN : MARGIN + side]
    middle = middle.at[:, :, :, :MARGIN].add(from_west)
    middle = middle.at[:, :, :, side - MARGIN :].add(from_east)
    from_south = from_behind(middle[:, :, :MARGIN, :], "row", -1)
    from_north = from_behind(middle[:, :, side + MARGIN :, :], "row", 1)
    core = middle[:, :, MARGIN : MARGIN + side, :]
    core = core.at[:, :, :MARGIN, :].add(from_north)
    core = core.at[:, :, side - MARGIN :, :].add(from_south)
    return core


def body(obj, probe, amplitude, positions):
    padded_object = padded(obj, (("row", 2), ("col", 3)), MARGIN)
    wide = padded_object.shape[2]
    table_re, table_im = tables(TILE)
    kernel_re, kernel_im = fresnel(TILE)
    spots = positions.reshape(-1, 2)
    count = spots.shape[0]
    measured = amplitude.reshape(count, TILE, TILE)

    def window(top_row, left_column):
        return lax.dynamic_slice(padded_object, (0, 0, top_row, left_column), (2, 2, TILE, TILE))

    patches = jax.vmap(window)(spots[:, 0], spots[:, 1])
    first = (1.0 + patches[:, 0, 0], patches[:, 0, 1])
    second = (1.0 + patches[:, 1, 0], patches[:, 1, 1])
    entry = cmul(probe[0], probe[1], first[0], first[1])
    spectrum = transform(entry, table_re, table_im)
    spectrum = cmul(kernel_re, kernel_im, spectrum[0], spectrum[1])
    inner = transform(spectrum, table_re, -table_im)
    leaving = cmul(inner[0], inner[1], second[0], second[1])
    far_re, far_im = transform(leaving, table_re, table_im)
    factor = measured / jnp.sqrt(far_re * far_re + far_im * far_im + 1.0)
    resid = (far_re - factor * far_re, far_im - factor * far_im)
    chi = transform(resid, table_re, -table_im)
    grad_two = cmul(inner[0], -inner[1], chi[0], chi[1])
    back = cmul(second[0], -second[1], chi[0], chi[1])
    back = transform(back, table_re, table_im)
    back = cmul(kernel_re, -kernel_im, back[0], back[1])
    back = transform(back, table_re, -table_im)
    grad_one = cmul(probe[0], -probe[1], back[0], back[1])
    grads = jnp.stack([jnp.stack(grad_one, 1), jnp.stack(grad_two, 1)], 1)

    def add_one(index, total):
        top_row = spots[index, 0]
        left_column = spots[index, 1]
        current = lax.dynamic_slice(total, (0, 0, top_row, left_column), (2, 2, TILE, TILE))
        return lax.dynamic_update_slice(total, current + grads[index], (0, 0, top_row, left_column))

    both_sum = margin_sum(
        lax.fori_loop(0, count, add_one, jnp.zeros((2, 2, wide, wide), jnp.float32))
    )
    return obj - step_size * both_sum


def solution(mesh):
    placed = (
        P(None, None, "row", "col"),
        P(),
        P("row", "col", None, None, None, None),
        P("row", "col", None, None, None),
    )
    return jax.shard_map(
        body, mesh=mesh, in_specs=placed, out_specs=P(None, None, "row", "col"), check_vma=False
    )
```

profile of v0, /device:TPU:33, one launch (start us, length us, event | category | flops | bytes accessed | tf_op | source)
XLA Modules:
  0.0 231.8 jit_solution(7394718620302653071)
XLA Ops:
  0.0 2.4 %fusion.50 = (f32[2,2,128,256]{3,2,1,0:T(8,128)}, f32[2,2,128,256]{3,2,1,0:T(8,128)}) fusion(f32[2,2,256,256]{3,2,1,0:T(8,128)} %param.14), kind=kLoop, calls=%fused_computation.136 | loop fusion | bytes 2097152 | tf_op jit(solution)/shard_map/slice | solution.py:26
  2.4 3.2 %collective-permute-start = (f32[2,2,128,256]{3,2,1,0:T(8,128)}, f32[2,2,128,256]{3,2,1,0:T(8,128)S(1)}, u32[]{:S(2)}, u32[]{:S(2)}) collective-permute-start(f32[2,2,128,256]{3,2,1,0:T(8,128)} %get-tuple-element.190), channel_id=1, source_target_pairs={{0,16},{16,32},{32,48},{48,64},{64,80},{80,96},{96,112},{112,128},... | collective-permute-start | bytes 1572872 | tf_op jit(solution)/shard_map/ppermute | solution.py:30
  5.6 1.9 collective-permute-start.1
  12.2 2.2 collective-permute-done
  14.5 5.1 %collective-permute-done.1 = f32[2,2,128,256]{3,2,1,0:T(8,128)S(1)} collective-permute-done((f32[2,2,128,256]{3,2,1,0:T(8,128)}, f32[2,2,128,256]{3,2,1,0:T(8,128)S(1)}, u32[]{:S(2)}, u32[]{:S(2)}) %collective-permute-start.1) | collective-permute-done | bytes 524320 | tf_op jit(solution)/shard_map/ppermute | solution.py:32
  19.8 5.0 %collective-permute-start.2 = (f32[2,2,512,128]{3,2,1,0:T(8,128)S(1)}, f32[2,2,512,128]{3,2,1,0:T(8,128)S(1)}, u32[]{:S(2)}, u32[]{:S(2)}) collective-permute-start(f32[2,2,512,128]{3,2,1,0:T(8,128)S(1)} %get-tuple-element.177), channel_id=1, source_target_pairs={{0,1},{1,2},{2,3},{3,4},{4,5},{5,6},{6,7},{7,8},{8,9},{9,10},{10,1... | collective-permute-start | bytes 3145736 | tf_op jit(solution)/shard_map/ppermute | solution.py:30
  28.4 1.9 fusion.38
  30.4 31.3 %collective-permute-done.2 = f32[2,2,512,128]{3,2,1,0:T(8,128)S(1)} collective-permute-done((f32[2,2,512,128]{3,2,1,0:T(8,128)S(1)}, f32[2,2,512,128]{3,2,1,0:T(8,128)S(1)}, u32[]{:S(2)}, u32[]{:S(2)}) %collective-permute-start.2) | collective-permute-done | bytes 1048608 | tf_op jit(solution)/shard_map/ppermute | solution.py:30
  61.6 9.4 %collective-permute-done.3 = f32[2,2,512,128]{3,2,1,0:T(8,128)S(1)} collective-permute-done((f32[2,2,512,128]{3,2,1,0:T(8,128)S(1)}, f32[2,2,512,128]{3,2,1,0:T(8,128)S(1)}, u32[]{:S(2)}, u32[]{:S(2)}) %collective-permute-start.3) | collective-permute-done | bytes 1048608 | tf_op jit(solution)/shard_map/ppermute | solution.py:32
  71.0 2.4 %pad_maximum_fusion = f32[2,2,512,512]{3,2,1,0:T(8,128)} fusion(f32[2,2,512,128]{3,2,1,0:T(8,128)S(1)} %collective-permute-done.3, f32[2,2,512,256]{3,2,1,0:T(8,128)S(1)} %constant_dynamic-update-slice_fusion.1, f32[2,2,512,128]{3,2,1,0:T(8,128)S(1)} %collective-permute-done.2), kind=kLoop, calls=%fused_computation.7 | loop fusion | flops 2097152 | bytes 8388608 | tf_op jit(solution)/shard_map/concatenate | solution.py:28
  73.4 10.3 %while.19 = (s32[]{:T(128)}, f32[2,2,512,512]{3,2,1,0:T(8,128)}, s32[2,4]{1,0:T(2,128)S(1)}, f32[2,2,2,256,256]{3,4,0,2,1:T(8,128)}, s32[]{:T(128)}) while((s32[]{:T(128)}, f32[2,2,512,512]{3,2,1,0:T(8,128)}, s32[2,4]{1,0:T(2,128)S(1)}, f32[2,2,2,256,256]{3,4,0,2,1:T(8,128)}, s32[]{:T(128)}) %tuple.86), condition=%wide.while_cond.4, body=%wide.while_body.4.sunk | while | flops 2 | bytes 6292089 | solution.py:95
  74.1 3.1 %dynamic-slice_bitcast_fusion.2 = f32[1,2,2,256,256]{4,3,2,1,0:T(8,128)S(1)} fusion(f32[2,2,512,512]{3,2,1,0:T(8,128)} %get-tuple-element.276, s32[]{:T(128)} %bitcast.232, s32[]{:T(128)} %bitcast.233), kind=kLoop, calls=%fused_computation.4.clone.1 | loop fusion | bytes 2097160 | tf_op jit(solution)/shard_map/vmap()/gather
  79.2 3.1 %dynamic-slice_bitcast_fusion.2 = f32[1,2,2,256,256]{4,3,2,1,0:T(8,128)S(1)} fusion(f32[2,2,512,512]{3,2,1,0:T(8,128)} %get-tuple-element.276, s32[]{:T(128)} %bitcast.232, s32[]{:T(128)} %bitcast.233), kind=kLoop, calls=%fused_computation.4.clone.1 | loop fusion | bytes 2097160 | tf_op jit(solution)/shard_map/vmap()/gather
  85.2 1.9 convolution_bitcast_fusion.11
  87.1 1.9 convolution_bitcast_fusion.10
  89.2 1.9 convolution_bitcast_fusion.9
  95.0 2.1 convolution_bitcast_fusion.6
  97.3 1.9 convolution_bitcast_fusion.5
  101.5 1.9 convolution_bitcast_fusion.3
  103.3 1.9 convolution_bitcast_fusion.2
  105.4 1.9 convolution_bitcast_fusion.1
  107.3 2.1 convolution_bitcast_fusion
  111.3 2.5 %broadcast_in_dim.2 = f32[2,2,512,512]{3,2,1,0:T(8,128)} broadcast(f32[]{:T(128)} %constant.167.clone.1), dimensions={} | broadcast | bytes 4194308 | tf_op jit(solution)/shard_map/broadcast_in_dim | solution.py:124
  113.8 39.5 %while.18 = (s32[]{:T(128)}, f32[2,2,512,512]{3,2,1,0:T(8,128)}, s32[2,2]{1,0:T(2,128)S(1)}, f32[2,2,2,256,256]{3,4,0,2,1:T(8,128)}, s32[]{:T(128)}, /*index=5*/s32[]{:T(128)}, s32[]{:T(128)}) while((s32[]{:T(128)}, f32[2,2,512,512]{3,2,1,0:T(8,128)}, s32[2,2]{1,0:T(2,128)S(1)}, f32[2,2,2,256,256]{3,4,0,2,1:T(8,128)}, s32[]{:T(128)}, ...), condition=%wide.region_1.2_spmd, body=%wide.region_0.1_spmd.sunk | while | flops 262152 | bytes 9437365 | solution.py:124
  121.7 12.2 %dynamic_update_slice.8 = f32[2,2,512,512]{3,2,1,0:T(8,128)} dynamic-update-slice(f32[2,2,512,512]{3,2,1,0:T(8,128)} %get-tuple-element.288, f32[2,2,256,256]{3,2,1,0:T(8,128)S(1)} %bitcast_add_fusion.2, s32[]{:T(128)} %constant.166.clone.1..sunk, s32[]{:T(128)} %constant.166.clone.1..sunk, s32[]{:T(128)S(6)} %select_n.156, s32[]{:T(128)S(6)} %select_n.157) | dynamic-update-slice | bytes 2097156 | tf_op jit(solution)/shard_map/while/body/eval_jaxpr/dynamic_update_slice | solution.py:121
  141.8 11.6 %dynamic_update_slice.8 = f32[2,2,512,512]{3,2,1,0:T(8,128)} dynamic-update-slice(f32[2,2,512,512]{3,2,1,0:T(8,128)} %get-tuple-element.288, f32[2,2,256,256]{3,2,1,0:T(8,128)S(1)} %bitcast_add_fusion.2, s32[]{:T(128)} %constant.166.clone.1..sunk, s32[]{:T(128)} %constant.166.clone.1..sunk, s32[]{:T(128)S(6)} %select_n.156, s32[]{:T(128)S(6)} %select_n.157) | dynamic-update-slice | bytes 2097156 | tf_op jit(solution)/shard_map/while/body/eval_jaxpr/dynamic_update_slice | solution.py:121
  155.2 2.0 collective-permute-start.4
  158.7 33.8 %collective-permute-done.4 = f32[2,2,512,128]{3,2,1,0:T(8,128)S(1)} collective-permute-done((f32[2,2,512,128]{3,2,1,0:T(8,128)S(1)}, f32[2,2,512,128]{3,2,1,0:T(8,128)S(1)}, u32[]{:S(2)}, u32[]{:S(2)}) %collective-permute-start.4) | collective-permute-done | bytes 1048608 | tf_op jit(solution)/shard_map/ppermute | solution.py:19
  193.0 26.1 %collective-permute-start.6 = (f32[2,2,128,256]{3,2,1,0:T(8,128)S(1)}, f32[2,2,128,256]{3,2,1,0:T(8,128)S(1)}, u32[]{:S(2)}, u32[]{:S(2)}) collective-permute-start(f32[2,2,128,256]{3,2,1,0:T(8,128)S(1)} %get-tuple-element.174), channel_id=1, source_target_pairs={{0,16},{16,32},{32,48},{48,64},{64,80},{80,96},{96,112},{112,128},... | collective-permute-start | bytes 1572872 | tf_op jit(solution)/shard_map/ppermute | solution.py:19
  219.1 1.9 collective-permute-start.7
  221.2 4.1 %collective-permute-done.6 = f32[2,2,128,256]{3,2,1,0:T(8,128)S(1)} collective-permute-done((f32[2,2,128,256]{3,2,1,0:T(8,128)S(1)}, f32[2,2,128,256]{3,2,1,0:T(8,128)S(1)}, u32[]{:S(2)}, u32[]{:S(2)}) %collective-permute-start.6) | collective-permute-done | bytes 524320 | tf_op jit(solution)/shard_map/ppermute | solution.py:19
  225.3 5.2 %collective-permute-done.7 = f32[2,2,128,256]{3,2,1,0:T(8,128)S(1)} collective-permute-done((f32[2,2,128,256]{3,2,1,0:T(8,128)S(1)}, f32[2,2,128,256]{3,2,1,0:T(8,128)S(1)}, u32[]{:S(2)}, u32[]{:S(2)}) %collective-permute-start.7) | collective-permute-done | bytes 524320 | tf_op jit(solution)/shard_map/ppermute | solution.py:19
  (87 shorter events, 35.7 us)
Async XLA Ops:
  0.0 7.5 %copy-start.11 = (f32[2,256,256]{2,1,0:T(8,128)S(1)}, f32[2,256,256]{2,1,0:T(8,128)}, u32[]{:S(2)}) copy-start(f32[2,256,256]{2,1,0:T(8,128)} %param.15) | copy-start | bytes 1572868
  0.0 9.3 %copy-start.12 = (f32[1,1,2,1,256,256]{5,4,3,2,1,0:T(8,128)S(1)}, f32[1,1,2,1,256,256]{5,4,3,2,1,0:T(8,128)}, u32[]{:S(2)}) copy-start(f32[1,1,2,1,256,256]{5,4,3,2,1,0:T(8,128)} %param.16) | copy-start | bytes 1572868
  2.4 12.0 %collective-permute-start = (f32[2,2,128,256]{3,2,1,0:T(8,128)}, f32[2,2,128,256]{3,2,1,0:T(8,128)S(1)}, u32[]{:S(2)}, u32[]{:S(2)}) collective-permute-start(f32[2,2,128,256]{3,2,1,0:T(8,128)} %get-tuple-element.190), channel_id=1, source_target_pairs={{0,16},{16,32},{32,48},{48,64},{64,80},{80,96},{96,112},{112,128},... | collective-permute-start | bytes 1572872 | tf_op jit(solution)/shard_map/ppermute | solution.py:30
  5.6 14.0 %collective-permute-start.1 = (f32[2,2,128,256]{3,2,1,0:T(8,128)}, f32[2,2,128,256]{3,2,1,0:T(8,128)S(1)}, u32[]{:S(2)}, u32[]{:S(2)}) collective-permute-start(f32[2,2,128,256]{3,2,1,0:T(8,128)} %get-tuple-element.189), channel_id=1, source_target_pairs={{16,0},{32,16},{48,32},{64,48},{80,64},{96,80},{112,96},{128,112},... | collective-permute-start | bytes 1572872 | tf_op jit(solution)/shard_map/ppermute | solution.py:32
  7.6 6.8 %copy-start.3 = (f32[2,2,256,256]{3,2,1,0:T(8,128)S(1)}, f32[2,2,256,256]{3,2,1,0:T(8,128)}, u32[]{:S(2)}) copy-start(f32[2,2,256,256]{3,2,1,0:T(8,128)} %param.14) | copy-start | bytes 3145732
  19.8 8.5 %copy-start.13 = (s32[1,1,2,1,2]{4,3,2,1,0:T(1,128)S(1)}, s32[1,1,2,1,2]{4,3,2,1,0:T(1,128)}, u32[]{:S(2)}) copy-start(s32[1,1,2,1,2]{4,3,2,1,0:T(1,128)} %param.17) | copy-start | bytes 52
  19.8 41.8 %collective-permute-start.2 = (f32[2,2,512,128]{3,2,1,0:T(8,128)S(1)}, f32[2,2,512,128]{3,2,1,0:T(8,128)S(1)}, u32[]{:S(2)}, u32[]{:S(2)}) collective-permute-start(f32[2,2,512,128]{3,2,1,0:T(8,128)S(1)} %get-tuple-element.177), channel_id=1, source_target_pairs={{0,1},{1,2},{2,3},{3,4},{4,5},{5,6},{6,7},{7,8},{8,9},{9,10},{10,1... | collective-permute-start | bytes 3145736 | tf_op jit(solution)/shard_map/ppermute | solution.py:30
  24.8 46.2 %collective-permute-start.3 = (f32[2,2,512,128]{3,2,1,0:T(8,128)S(1)}, f32[2,2,512,128]{3,2,1,0:T(8,128)S(1)}, u32[]{:S(2)}, u32[]{:S(2)}) collective-permute-start(f32[2,2,512,128]{3,2,1,0:T(8,128)S(1)} %get-tuple-element.178), channel_id=1, source_target_pairs={{1,0},{2,1},{3,2},{4,3},{5,4},{6,5},{7,6},{8,7},{9,8},{10,9},{11,1... | collective-permute-start | bytes 3145736 | tf_op jit(solution)/shard_map/ppermute | solution.py:32
  85.2 1.9 copy-start.1
  85.2 1.9 copy-start.2
  87.1 1.9 copy-start.9
  91.1 1.9 copy-start.5
  95.0 2.1 copy-start.7
  103.3 1.9 copy-start.8
  107.3 2.2 copy-start.6
  107.3 2.2 copy-start.10
  153.3 5.1 %copy-start = (f32[2,2,512,512]{3,2,1,0:T(8,128)S(1)}, f32[2,2,512,512]{3,2,1,0:T(8,128)}, u32[]{:S(2)}) copy-start(f32[2,2,512,512]{3,2,1,0:T(8,128)} %get-tuple-element.132) | copy-start | bytes 12582916
  155.2 37.3 %collective-permute-start.4 = (f32[2,2,512,128]{3,2,1,0:T(8,128)S(1)}, f32[2,2,512,128]{3,2,1,0:T(8,128)S(1)}, u32[]{:S(2)}, u32[]{:S(2)}) collective-permute-start(f32[2,2,512,128]{3,2,1,0:T(8,128)S(1)} %get-tuple-element.166), channel_id=1, source_target_pairs={{0,1},{1,2},{2,3},{3,4},{4,5},{5,6},{6,7},{7,8},{8,9},{9,10},{10,1... | collective-permute-start | bytes 3145736 | tf_op jit(solution)/shard_map/ppermute | solution.py:19
  157.2 35.6 %collective-permute-start.5 = (f32[2,2,512,128]{3,2,1,0:T(8,128)S(1)}, f32[2,2,512,128]{3,2,1,0:T(8,128)S(1)}, u32[]{:S(2)}, u32[]{:S(2)}) collective-permute-start(f32[2,2,512,128]{3,2,1,0:T(8,128)S(1)} %get-tuple-element.165), channel_id=1, source_target_pairs={{1,0},{2,1},{3,2},{4,3},{5,4},{6,5},{7,6},{8,7},{9,8},{10,9},{11,1... | collective-permute-start | bytes 3145736 | tf_op jit(solution)/shard_map/ppermute | solution.py:19
  193.0 32.2 %collective-permute-start.6 = (f32[2,2,128,256]{3,2,1,0:T(8,128)S(1)}, f32[2,2,128,256]{3,2,1,0:T(8,128)S(1)}, u32[]{:S(2)}, u32[]{:S(2)}) collective-permute-start(f32[2,2,128,256]{3,2,1,0:T(8,128)S(1)} %get-tuple-element.174), channel_id=1, source_target_pairs={{0,16},{16,32},{32,48},{48,64},{64,80},{80,96},{96,112},{112,128},... | collective-permute-start | bytes 1572872 | tf_op jit(solution)/shard_map/ppermute | solution.py:19
  219.1 11.4 %collective-permute-start.7 = (f32[2,2,128,256]{3,2,1,0:T(8,128)S(1)}, f32[2,2,128,256]{3,2,1,0:T(8,128)S(1)}, u32[]{:S(2)}, u32[]{:S(2)}) collective-permute-start(f32[2,2,128,256]{3,2,1,0:T(8,128)S(1)} %get-tuple-element.173), channel_id=1, source_target_pairs={{16,0},{32,16},{48,32},{64,48},{80,64},{96,80},{112,96},{128,112},... | collective-permute-start | bytes 1572872 | tf_op jit(solution)/shard_map/ppermute | solution.py:19
  221.2 9.5 %copy-start.4 = (f32[2,2,256,256]{3,2,1,0:T(8,128)S(1)}, f32[2,2,256,256]{3,2,1,0:T(8,128)}, u32[]{:S(2)}) copy-start(f32[2,2,256,256]{3,2,1,0:T(8,128)} %param.14) | copy-start | bytes 3145732
where the time goes:
time: 233 us; the launch traced here: 232 us
  waiting for transfers between devices  91 us (39%)
  local copies, waits for them, and re-layouts  49.5 us (21%)
  starting transfers between devices  42.7 us (18%)
  matrix products  23.1 us (10%)
  other arithmetic  17.2 us (7%)
  loops' own time  7.77 us (3%)
    ppermute x4, waiting for transfers between devices, from_behind(): lax.ppermute(value, axis, [(source, source + steps) for source in range(i...  43.1 us
    ppermute x2, waiting for transfers between devices, padded(): lax.ppermute(tail, axis, [(i, (i + 1) % count) for i in range(ends)])  33.4 us
    ppermute x4, starting transfers between devices, from_behind(): lax.ppermute(value, axis, [(source, source + steps) for source in range(i...  31.3 us
    dynamic_update_slice x2, local copies, waits for them, and re-layouts, add_one(): lax.dynamic_update_slice(total, current + grads[index], (0, 0, top_row, l...  23.8 us
    ppermute x2, waiting for transfers between devices, padded(): lax.ppermute(head, axis, [((i + 1) % count, i) for i in range(ends)])  14.5 us
    dot_general x6, matrix products, transform(): out = jnp.einsum('dbkj,djcl->cbkl', left, right_block, precision=highest)  11.7 us
    dot_general x6, matrix products, transform(): left = jnp.einsum('ckdj,dbjl->cbkl', block, stacked, precision=highest)  11.4 us
    gather x10, local copies, waits for them, and re-layouts  10.3 us
  transfers between devices with their start and end apart: 8, of which 7 were waited for; matrix products, arithmetic and copies ran while one was open for 4% of the time, Pallas kernels for 0%

commit v1 on v0

v1 whole, which is shorter than its diff:
```python
import functools
import math

import jax
import jax.numpy as jnp
import numpy as np
from jax import lax
from jax.experimental import pallas as pl
from jax.experimental.pallas import tpu as pltpu
from jax.sharding import PartitionSpec as P

TILE = 256
MARGIN = 128
HALF = 128
WIDE = 512
STEP = 0.5
MESH = pl.DeviceIdType.MESH

G_FX, G_FI, G_VX, G_VI, G_CROSS, G_CROSS2, G_DIRECT, G_FWD, G_IN, G_IN2, G_INF, G_INV = range(12)
S_CROSS, S_DIRECT, S_IN, S_FX, S_FI, S_VX, S_VI = range(7)

T_A, T_F, T_FI, T_AC = range(4)


def real_form(m):
    return np.block([[m.real, m.imag], [-m.imag, m.real]])


def matrices():
    n = np.arange(TILE)
    f = np.where(n < TILE // 2, n, n - TILE)
    h = np.exp(-1j * math.pi * ((f * f) % (4 * TILE)) / (2 * TILE))
    dft = np.exp(-2j * math.pi * ((n[:, None] * n[None, :]) % TILE) / TILE) / math.sqrt(TILE)
    spread = np.conj(dft) @ (h[:, None] * dft)
    c0, c1 = spread[:HALF, :HALF], spread[:HALF, HALF:]
    a = [(c0 + c1) / 2, (c0 - c1) / 2]
    fwd = [dft[:HALF, 0::2], dft[:HALF, 1::2]]
    inv = [np.conj(m.T) for m in fwd]
    ac = [np.conj(m) for m in a]
    return np.stack([np.stack([real_form(m) for m in pair]) for pair in (a, fwd, inv, ac)])


def constants():
    right = matrices()
    both = np.stack([right, np.swapaxes(right, -1, -2)], 2)
    both = both.astype(np.float32)
    high = both.astype(jnp.bfloat16)
    low = (both - high.astype(np.float32)).astype(jnp.bfloat16)
    mats = np.stack([high, low], 3)
    order = np.concatenate([np.arange(0, TILE, 2), np.arange(1, TILE, 2)])
    perm = np.zeros((TILE, TILE), np.float32)
    perm[order, np.arange(TILE)] = 1.0
    perms = np.stack([perm, perm.T]).astype(jnp.bfloat16)
    return mats, perms


def split(x):
    high = x.astype(jnp.bfloat16)
    low = (x - high.astype(jnp.float32)).astype(jnp.bfloat16)
    return high, low


def dot(a, b):
    return jnp.dot(a, b, preferred_element_type=jnp.float32)


def mm_right(x, high, low):
    xh, xl = split(x)
    return dot(xh, high) + (dot(xl, high) + dot(xh, low))


def mm_left(high, low, x):
    xh, xl = split(x)
    return dot(high, xh) + (dot(high, xl) + dot(low, xh))


def transform(src, mid, dst, mats, which, pre, post):
    def one(w, carry):
        xr, xi = src[w, 0], src[w, 1]
        r0, r1, i0, i1 = xr[:, :HALF], xr[:, HALF:], xi[:, :HALF], xi[:, HALF:]
        if pre:
            r0, r1, i0, i1 = r0 + r1, r0 - r1, i0 + i1, i0 - i1
        ys = mm_right(jnp.concatenate([r0, i0], 1), mats[which, 0, 0, 0], mats[which, 0, 0, 1])
        yd = mm_right(jnp.concatenate([r1, i1], 1), mats[which, 1, 0, 0], mats[which, 1, 0, 1])
        if post:
            ys, yd = ys + yd, ys - yd
        yr = jnp.concatenate([ys[:, :HALF], yd[:, :HALF]], 1)
        yi = jnp.concatenate([ys[:, HALF:], yd[:, HALF:]], 1)
        r0, r1, i0, i1 = yr[:HALF], yr[HALF:], yi[:HALF], yi[HALF:]
        if pre:
            r0, r1, i0, i1 = r0 + r1, r0 - r1, i0 + i1, i0 - i1
        zs = mm_left(mats[which, 0, 1, 0], mats[which, 0, 1, 1], jnp.concatenate([r0, i0], 0))
        zd = mm_left(mats[which, 1, 1, 0], mats[which, 1, 1, 1], jnp.concatenate([r1, i1], 0))
        if post:
            zs, zd = zs + zd, zs - zd
        dst[w, 0, :HALF, :] = zs[:HALF]
        dst[w, 0, HALF:, :] = zd[:HALF]
        dst[w, 1, :HALF, :] = zs[HALF:]
        dst[w, 1, HALF:, :] = zd[HALF:]
        return carry

    lax.fori_loop(0, 2, one, 0)


ROWS = 32


def rows_loop(count, fn):
    def step(k, carry):
        fn(pl.multiple_of(k * ROWS, ROWS))
        return carry

    lax.fori_loop(0, count // ROWS, step, 0)


def kernel(
    n_row, n_col,
    pos_ref, obj_ref, probe_ref, amp_ref, mats_ref, perms_ref,
    out_ref,
    pad0, pad1, tot0, tot1, gbuf, probe, amp, mats, perms, amp_p, x_ref, b_ref, t_ref, mid,
    r_in, r_x, r_d, r_f, r_v,
    local_sem, g_send, g_recv, s_send, s_recv,
):
    i, j = lax.axis_index("row"), lax.axis_index("col")
    core = lax.rem(i, 2)
    c = lax.rem(lax.div(i, 2), 2)
    i_in = i + 1 - 2 * core
    i_x = i - 1 + 2 * core
    j_v = j - 1 + 2 * c
    j_f = j + 1 - 2 * c
    has_x = jnp.logical_and(i_x >= 0, i_x < n_row)
    has_v = jnp.logical_and(j_v >= 0, j_v < n_col)
    has_f = jnp.logical_and(j_f >= 0, j_f < n_col)
    has_d = jnp.logical_and(has_x, has_v)
    ix = jnp.clip(i_x, 0, n_row - 1)
    jv = jnp.clip(j_v, 0, n_col - 1)
    jf = jnp.clip(j_f, 0, n_col - 1)
    always = None
    pads, tots = (pad0, pad1), (tot0, tot1)

    def at(start):
        return pl.ds(pl.multiple_of(start, HALF), HALF)

    x_rows, in_rows = at(HALF * core), at(HALF * (1 - core))
    x_rows_p, in_rows_p = at(MARGIN + HALF * core), at(MARGIN + HALF * (1 - core))

    border = jnp.logical_not(jnp.logical_and(has_x, jnp.logical_and(has_v, has_f)))

    @pl.when(border)
    def _():
        def zero(r):
            for pad in pads:
                pad[:, :, pl.ds(r, ROWS), :] = jnp.zeros((2, 4, ROWS, HALF), jnp.float32)

        rows_loop(WIDE, zero)

    barrier = pltpu.get_barrier_semaphore()

    def when(cond, fn):
        if cond is None:
            fn()
        else:
            pl.when(cond)(fn)

    partners = ((None, (i_in, j)), (has_x, (ix, j)), (has_d, (ix, jv)), (has_v, (i, jv)), (has_f, (i, jf)))
    for cond, dev in partners:
        when(cond, lambda dev=dev: pl.semaphore_signal(barrier, inc=1, device_id=dev, device_id_type=MESH))
    one = lambda cond: cond.astype(jnp.int32)
    pl.semaphore_wait(barrier, 1 + one(has_x) + one(has_d) + one(has_v) + one(has_f))

    def gather(s):
        pad = pads[s]
        dst_x, dst_in = at(3 * HALF * (1 - core)), at(3 * HALF * core)
        f_src, f_dst = at(HALF * (1 - c)), 3 * c
        v_src, v_dst = at(HALF * c), 3 * (1 - c)
        west, east = pl.ds(0, HALF), pl.ds(HALF, HALF)
        obj = obj_ref.at[s]
        table = {
            G_FX: (has_f, has_v, obj.at[:, x_rows, f_src], pad.at[:, f_dst, x_rows_p, :], (i, jf)),
            G_FI: (has_f, has_v, obj.at[:, in_rows, f_src], pad.at[:, f_dst, in_rows_p, :], (i, jf)),
            G_VX: (has_v, has_f, obj.at[:, x_rows, v_src], pad.at[:, v_dst, x_rows_p, :], (i, jv)),
            G_VI: (has_v, has_f, obj.at[:, in_rows, v_src], pad.at[:, v_dst, in_rows_p, :], (i, jv)),
            G_CROSS: (has_x, has_x, obj.at[:, x_rows, west], pad.at[:, 1, dst_x, :], (ix, j)),
            G_CROSS2: (has_x, has_x, obj.at[:, x_rows, east], pad.at[:, 2, dst_x, :], (ix, j)),
            G_DIRECT: (has_d, has_d, obj.at[:, x_rows, v_src], pad.at[:, v_dst, dst_x, :], (ix, jv)),
            G_FWD: (has_x, has_x, pad.at[:, f_dst, x_rows_p, :], pad.at[:, f_dst, dst_x, :], (ix, j)),
            G_IN: (always, always, obj.at[:, in_rows, west], pad.at[:, 1, dst_in, :], (i_in, j)),
            G_IN2: (always, always, obj.at[:, in_rows, east], pad.at[:, 2, dst_in, :], (i_in, j)),
            G_INF: (always, always, pad.at[:, f_dst, in_rows_p, :], pad.at[:, f_dst, dst_in, :], (i_in, j)),
            G_INV: (always, always, pad.at[:, v_dst, in_rows_p, :], pad.at[:, v_dst, dst_in, :], (i_in, j)),
        }
        return {
            k: (sent, comes, pltpu.make_async_remote_copy(
                src_ref=src, dst_ref=dst, send_sem=g_send.at[s, k], recv_sem=g_recv.at[s, k],
                device_id=dev, device_id_type=MESH))
            for k, (sent, comes, src, dst, dev) in table.items()
        }

    def start(copies, *keys):
        for k in keys:
            sent, _, copy = copies[k]
            when(sent, copy.start)

    def arrived(copies, *keys):
        for k in keys:
            _, comes, copy = copies[k]
            when(comes, copy.wait_recv)

    def left(copies, *keys):
        for k in keys:
            sent, _, copy = copies[k]
            when(sent, copy.wait_send)

    g0, g1 = gather(0), gather(1)
    first = (G_FX, G_CROSS, G_CROSS2, G_FI, G_VI, G_VX, G_DIRECT, G_IN, G_IN2)
    start(g0, *first)

    inner = pl.ds(MARGIN, TILE)
    locals_ = [
        pltpu.make_async_copy(obj_ref.at[s, :, :, pl.ds(HALF * k, HALF)], pad.at[:, 1 + k, inner, :], local_sem.at[4 + 2 * s + k])
        for s, pad in enumerate(pads)
        for k in range(2)
    ] + [
        pltpu.make_async_copy(probe_ref, probe, local_sem.at[0]),
        pltpu.make_async_copy(amp_ref, amp, local_sem.at[1]),
        pltpu.make_async_copy(mats_ref, mats, local_sem.at[2]),
        pltpu.make_async_copy(perms_ref, perms, local_sem.at[3]),
    ]
    for copy in locals_:
        copy.start()

    start(g1, *first)

    def clear(r):
        for w in range(2):
            gbuf[w, :, :, pl.ds(r, ROWS), :] = jnp.zeros((2, 5, ROWS, HALF), jnp.float32)

    rows_loop(3 * TILE, clear)
    for copy in locals_[5:]:
        copy.wait()

    def order(w, carry):
        rest = amp[w]
        total = None
        for _ in range(3):
            piece = rest.astype(jnp.bfloat16)
            rest = rest - piece.astype(jnp.float32)
            part = dot(perms[1], dot(piece, perms[0]).astype(jnp.bfloat16))
            total = part if total is None else total + part
        amp_p[w] = total
        return carry

    lax.fori_loop(0, 2, order, 0)
    for copy in locals_[:5]:
        copy.wait()

    lane = lax.broadcasted_iota(jnp.int32, (ROWS, HALF), 1)

    def place(w):
        y, x = pos_ref[2 * w], pos_ref[2 * w + 1]
        q = jnp.minimum(lax.div(x, HALF), 1)
        return y, q, x - q * HALF

    def window(pad, w, part, r):
        y, block, s = place(w)
        turn = lax.rem(HALF - s, HALF)
        v = [pltpu.roll(pad[part, block + k, pl.ds(y + r, ROWS), :], turn, 1) for k in range(3)]
        own = lane < HALF - s
        return jnp.concatenate([jnp.where(own, v[0], v[1]), jnp.where(own, v[1], v[2])], 1)

    def finish_gather(copies):
        arrived(copies, G_FX)
        start(copies, G_FWD)
        arrived(copies, G_FI)
        start(copies, G_INF)
        arrived(copies, G_VI)
        start(copies, G_INV)
        arrived(copies, G_VX, G_CROSS, G_CROSS2, G_DIRECT, G_IN, G_IN2, G_FWD, G_INF, G_INV)

    finish_gather(g0)

    for w in range(2):
        def enter(r, w=w):
            rows = pl.ds(r, ROWS)
            tr, ti = 1.0 + window(pad0, w, 0, r), window(pad0, w, 1, r)
            pr, pi = probe[0, rows, :], probe[1, rows, :]
            x_ref[w, 0, rows, :] = pr * tr - pi * ti
            x_ref[w, 1, rows, :] = pr * ti + pi * tr

        rows_loop(TILE, enter)
    transform(x_ref, mid, b_ref, mats, T_A, True, True)

    finish_gather(g1)

    for w in range(2):
        def leave(r, w=w):
            rows = pl.ds(r, ROWS)
            tr, ti = 1.0 + window(pad1, w, 0, r), window(pad1, w, 1, r)
            t_ref[w, 0, rows, :] = tr
            t_ref[w, 1, rows, :] = ti
            br, bi = b_ref[w, 0, rows, :], b_ref[w, 1, rows, :]
            x_ref[w, 0, rows, :] = br * tr - bi * ti
            x_ref[w, 1, rows, :] = br * ti + bi * tr

        rows_loop(TILE, leave)
    transform(x_ref, mid, x_ref, mats, T_F, True, False)

    for w in range(2):
        def residual(r, w=w):
            rows = pl.ds(r, ROWS)
            fr, fi = x_ref[w, 0, rows, :], x_ref[w, 1, rows, :]
            keep = 1.0 - amp_p[w, rows, :] * lax.rsqrt(fr * fr + fi * fi + 1.0)
            x_ref[w, 0, rows, :] = fr * keep
            x_ref[w, 1, rows, :] = fi * keep

        rows_loop(TILE, residual)
    transform(x_ref, mid, x_ref, mats, T_FI, False, True)

    def turned(w, part, r, v):
        _, _, s = place(w)
        turn = lax.rem(s, HALF)
        a, b = (pltpu.roll(v[:, HALF * k : HALF * (k + 1)], turn, 1) for k in range(2))
        own = lane >= s
        rows = pl.ds(TILE + r, ROWS)
        gbuf[w, part, 1, rows, :] = jnp.where(own, a, 0.0)
        gbuf[w, part, 2, rows, :] = jnp.where(own, b, a)
        gbuf[w, part, 3, rows, :] = jnp.where(own, 0.0, b)

    def add_up(tot):
        def chunk(r):
            for part in range(2):
                for k in range(4):
                    total = None
                    for w in range(2):
                        y, block, _ = place(w)
                        v = gbuf[w, part, 1 - block + k, pl.ds(TILE - y + r, ROWS), :]
                        total = v if total is None else total + v
                    tot[part, k, pl.ds(r, ROWS), :] = total

        rows_loop(WIDE, chunk)

    def scatter(s):
        tot = tots[s]
        cross_rows, inner_rows = at(3 * HALF * core), at(3 * HALF * (1 - core))
        f_blk, v_blk = 3 * (1 - c), 3 * c
        table = {
            S_CROSS: (has_x, has_x, tot.at[:, pl.ds(1 - c, 3), cross_rows, :], r_x.at[s], (ix, j)),
            S_DIRECT: (has_d, has_d, tot.at[:, v_blk, cross_rows, :], r_d.at[s], (ix, jv)),
            S_IN: (always, always, tot.at[:, :, inner_rows, :], r_in.at[s], (i_in, j)),
            S_FX: (has_f, has_v, tot.at[:, f_blk, x_rows_p, :], r_f.at[s, :, x_rows, :], (i, jf)),
            S_FI: (has_f, has_v, tot.at[:, f_blk, in_rows_p, :], r_f.at[s, :, in_rows, :], (i, jf)),
            S_VX: (has_v, has_f, tot.at[:, v_blk, x_rows_p, :], r_v.at[s, :, x_rows, :], (i, jv)),
            S_VI: (has_v, has_f, tot.at[:, v_blk, in_rows_p, :], r_v.at[s, :, in_rows, :], (i, jv)),
        }
        return {
            k: (sent, comes, pltpu.make_async_remote_copy(
                src_ref=src, dst_ref=dst, send_sem=s_send.at[s, k], recv_sem=s_recv.at[s, k],
                device_id=dev, device_id_type=MESH))
            for k, (sent, comes, src, dst, dev) in table.items()
        }

    def add_in(s):
        tot = tots[s]

        def chunk(r):
            rows = pl.ds(pl.multiple_of(MARGIN + HALF * (1 - core) + r, ROWS), ROWS)
            tot[:, :, rows, :] = tot[:, :, rows, :] + r_in[s, :, :, pl.ds(r, ROWS), :]

        rows_loop(HALF, chunk)

    def add_cross(s):
        tot = tots[s]
        blks = pl.ds(c, 3)

        def chunk(r):
            rows = pl.ds(pl.multiple_of(MARGIN + HALF * core + r, ROWS), ROWS)
            tot[:, blks, rows, :] = tot[:, blks, rows, :] + r_x[s, :, :, pl.ds(r, ROWS), :]

        @pl.when(has_x)
        def _():
            rows_loop(HALF, chunk)

    def send_early(s, copies):
        start(copies, S_CROSS, S_IN, S_FX, S_DIRECT)

    def send_inner(s, copies):
        arrived(copies, S_IN)
        add_in(s)
        start(copies, S_FI, S_VI)

    def send_late(s, copies):
        arrived(copies, S_CROSS)
        add_cross(s)
        start(copies, S_VX)

    def finish(s, copies):
        tot = tots[s]
        arrived(copies, S_DIRECT, S_FX, S_FI, S_VX, S_VI)

        def add(cond, count, first_row, blk, buf):
            def chunk(r):
                rows = pl.ds(pl.multiple_of(first_row + r, ROWS), ROWS)
                tot[:, blk, rows, :] = tot[:, blk, rows, :] + buf[s, :, pl.ds(r, ROWS), :]

            @pl.when(cond)
            def _():
                rows_loop(count, chunk)

        add(has_d, HALF, MARGIN + HALF * core, 1 + c, r_d)
        add(has_v, TILE, MARGIN, 1 + c, r_f)
        add(has_f, TILE, MARGIN, 2 - c, r_v)

        def chunk(r):
            for k in range(2):
                out_ref[s, :, pl.ds(r, ROWS), HALF * k : HALF * (k + 1)] = tot[:, 1 + k, pl.ds(MARGIN + r, ROWS), :]

        rows_loop(TILE, chunk)

    for w in range(2):
        def second(r, w=w):
            rows = pl.ds(r, ROWS)
            br, bi = b_ref[w, 0, rows, :], b_ref[w, 1, rows, :]
            cr, ci = x_ref[w, 0, rows, :], x_ref[w, 1, rows, :]
            turned(w, 0, r, br * cr + bi * ci)
            turned(w, 1, r, br * ci - bi * cr)

        rows_loop(TILE, second)
    add_up(tot1)
    s1 = scatter(1)
    send_early(1, s1)

    for w in range(2):
        def back(r, w=w):
            rows = pl.ds(r, ROWS)
            tr, ti = t_ref[w, 0, rows, :], t_ref[w, 1, rows, :]
            cr, ci = x_ref[w, 0, rows, :], x_ref[w, 1, rows, :]
            x_ref[w, 0, rows, :] = tr * cr + ti * ci
            x_ref[w, 1, rows, :] = tr * ci - ti * cr

        rows_loop(TILE, back)
    send_inner(1, s1)
    transform(x_ref, mid, x_ref, mats, T_AC, True, True)
    for w in range(2):
        def first_slice(r, w=w):
            rows = pl.ds(r, ROWS)
            pr, pi = probe[0, rows, :], probe[1, rows, :]
            cr, ci = x_ref[w, 0, rows, :], x_ref[w, 1, rows, :]
            turned(w, 0, r, pr * cr + pi * ci)
            turned(w, 1, r, pr * ci - pi * cr)

        rows_loop(TILE, first_slice)
    add_up(tot0)
    s0 = scatter(0)
    send_early(0, s0)
    send_inner(0, s0)
    send_late(1, s1)
    send_late(0, s0)
    finish(1, s1)
    finish(0, s0)
    for copies in (g0, g1, s0, s1):
        left(copies, *copies)


def body(n_row, n_col, mats, perms, obj, probe, amplitude, positions):
    any_space = pl.BlockSpec(memory_space=pl.ANY)
    vmem = pl.BlockSpec(memory_space=pltpu.VMEM)
    smem = pl.BlockSpec(memory_space=pltpu.SMEM)
    f32 = jnp.float32
    wide = pltpu.VMEM((2, 4, WIDE, HALF), f32)
    field = pltpu.VMEM((2, 2, TILE, TILE), f32)
    gradient = pl.pallas_call(
        functools.partial(kernel, n_row, n_col),
        out_shape=jax.ShapeDtypeStruct((2, 2, TILE, TILE), f32),
        in_specs=[smem] + [any_space] * 5,
        out_specs=vmem,
        scratch_shapes=[
            wide, wide, wide, wide,
            pltpu.VMEM((2, 2, 5, 3 * TILE, HALF), f32),
            pltpu.VMEM((2, TILE, TILE), f32),
            pltpu.VMEM((2, TILE, TILE), f32),
            pltpu.VMEM(mats.shape, jnp.bfloat16),
            pltpu.VMEM(perms.shape, jnp.bfloat16),
            pltpu.VMEM((2, TILE, TILE), f32),
            field, field, field,
            pltpu.VMEM((2, TILE, TILE), f32),
            pltpu.VMEM((2, 2, 4, HALF, HALF), f32),
            pltpu.VMEM((2, 2, 3, HALF, HALF), f32),
            pltpu.VMEM((2, 2, HALF, HALF), f32),
            pltpu.VMEM((2, 2, TILE, HALF), f32),
            pltpu.VMEM((2, 2, TILE, HALF), f32),
            pltpu.SemaphoreType.DMA((8,)),
            pltpu.SemaphoreType.DMA((2, 12)),
            pltpu.SemaphoreType.DMA((2, 12)),
            pltpu.SemaphoreType.DMA((2, 7)),
            pltpu.SemaphoreType.DMA((2, 7)),
        ],
        compiler_params=pltpu.CompilerParams(
            collective_id=0, has_side_effects=True, vmem_limit_bytes=56 * 1024 * 1024
        ),
        cost_estimate=pl.CostEstimate(flops=3 * 10**9, bytes_accessed=8 * 10**6, transcendentals=131072),
    )(positions.reshape(4), obj, probe, amplitude.reshape(2, TILE, TILE), mats, perms)
    return obj - STEP * gradient


def solution(mesh):
    mats, perms = constants()
    mats, perms = jnp.asarray(mats), jnp.asarray(perms)
    placed = (
        P(None, None, "row", "col"),
        P(),
        P("row", "col", None, None, None, None),
        P("row", "col", None, None, None),
    )
    return jax.shard_map(
        functools.partial(body, mesh.shape["row"], mesh.shape["col"], mats, perms),
        mesh=mesh, in_specs=placed, out_specs=P(None, None, "row", "col"), check_vma=False,
    )
```

time: 233 us -> 111 us (0.48)
  the two profiles are of different devices: /device:TPU:33 before, /device:TPU:26 now
where the time goes in v1:
time: 111 us; the launch traced here: 110 us
  Pallas kernels  105 us (95%)
  other arithmetic  3.67 us (3%)
  local copies, waits for them, and re-layouts  1.11 us (1%)
    pallas_call x1, Pallas kernels, body(): pl.pallas_call(functools.partial(kernel, n_row, n_col), out_shape=jax.Sha...  105 us
    sub x1, other arithmetic, body(): return obj - STEP * gradient  2.33 us

profile of v1, /device:TPU:26, one launch (start us, length us, event | category | flops | bytes accessed | tf_op | source)
XLA Modules:
  0.0 109.8 jit_solution(3496013090803762316)
XLA Ops:
  0.0 0.5 broadcast.3
  0.5 1.3 %reduce.3 = s32[2,2]{1,0:T(2,128)S(1)} reduce(s32[1,1,2,1,2]{4,3,2,1,0:T(1,128)} %param.9, s32[]{:T(128)} %broadcast.3), dimensions={0,1,3}, to_apply=%param.9.reduce_sub_computation.3 | reduce | bytes 36 | tf_op args[3]
  1.9 0.6 reshape.6.pos_ref
  2.4 0.0 copy-start
  2.4 105.0 %shard_map.64 = f32[2,2,256,256]{3,2,1,0:T(8,128)} custom-call(s32[4]{0:T(128)} %reshape.6.pos_ref, f32[2,2,256,256]{3,2,1,0:T(8,128)} %obj_ref.1, f32[2,256,256]{2,1,0:T(8,128)} %probe_ref.1, f32[2,256,256]{2,1,0:T(8,128)} %bitcast.1, bf16[4,2,2,2,256,256]{5,4,3,2,1,0:T(8,128)(2,1)} %constant.6.clone.mats_ref, bf16[2,256,256]{2,1,0:T(8,128)(2,1)} %constant.7.clone.perms_ref), custom_call_target="tpu_custom_call" | custom-call | flops 3000000000 | bytes 8000000 | tf_op jit(solution)/shard_map/pallas_call | solution.py:471
  107.5 0.0 copy-done
  107.5 2.3 %multiply_subtract_fusion = f32[2,2,256,256]{3,2,1,0:T(8,128)} fusion(f32[2,2,256,256]{3,2,1,0:T(8,128)S(1)} %copy-done, f32[2,2,256,256]{3,2,1,0:T(8,128)} %shard_map.64), kind=kLoop, calls=%fused_computation | loop fusion | flops 524288 | bytes 3145728 | tf_op jit(solution)/shard_map/sub | solution.py:502
Async XLA Ops:
  2.4 105.1 %copy-start = (f32[2,2,256,256]{3,2,1,0:T(8,128)S(1)}, f32[2,2,256,256]{3,2,1,0:T(8,128)}, u32[]{:S(2)}) copy-start(f32[2,2,256,256]{3,2,1,0:T(8,128)} %obj_ref.1) | copy-start | bytes 3145732

commit v2 on v1

--- a/solution.py
+++ b/solution.py
@@ -17,7 +17,7 @@
 MESH = pl.DeviceIdType.MESH
 
 G_FX, G_FI, G_VX, G_VI, G_CROSS, G_CROSS2, G_DIRECT, G_FWD, G_IN, G_IN2, G_INF, G_INV = range(12)
-S_CROSS, S_DIRECT, S_IN, S_FX, S_FI, S_VX, S_VI = range(7)
+S_CORNER, S_CROSS, S_DIRECT, S_IN, S_FX, S_FI, S_VX, S_VI = range(8)
 
 T_A, T_F, T_FI, T_AC = range(4)
 
@@ -74,7 +74,7 @@
     return dot(high, xh) + (dot(high, xl) + dot(low, xh))
 
 
-def transform(src, mid, dst, mats, which, pre, post):
+def transform(src, dst, mats, which, pre, post):
     def one(w, carry):
         xr, xi = src[w, 0], src[w, 1]
         r0, r1, i0, i1 = xr[:, :HALF], xr[:, HALF:], xi[:, :HALF], xi[:, HALF:]
@@ -117,8 +117,8 @@
     n_row, n_col,
     pos_ref, obj_ref, probe_ref, amp_ref, mats_ref, perms_ref,
     out_ref,
-    pad0, pad1, tot0, tot1, gbuf, probe, amp, mats, perms, amp_p, x_ref, b_ref, t_ref, mid,
-    r_in, r_x, r_d, r_f, r_v,
+    pad0, pad1, tot0, tot1, gbuf, probe, amp, mats, perms, amp_p, x_ref, b_ref, t_ref,
+    r_in, r_x, r_c, r_d, r_f, r_v,
     local_sem, g_send, g_recv, s_send, s_recv,
 ):
     i, j = lax.axis_index("row"), lax.axis_index("col")
@@ -212,8 +212,10 @@
             when(sent, copy.wait_send)
 
     g0, g1 = gather(0), gather(1)
-    first = (G_FX, G_CROSS, G_CROSS2, G_FI, G_VI, G_VX, G_DIRECT, G_IN, G_IN2)
-    start(g0, *first)
+    rest = (G_IN, G_IN2, G_CROSS, G_CROSS2, G_FI, G_VI, G_VX, G_DIRECT)
+    start(g0, G_FX)
+    start(g1, G_FX)
+    start(g0, *rest)
 
     inner = pl.ds(MARGIN, TILE)
     locals_ = [
@@ -229,7 +231,7 @@
     for copy in locals_:
         copy.start()
 
-    start(g1, *first)
+    start(g1, *rest)
 
     def clear(r):
         for w in range(2):
@@ -257,7 +259,7 @@
     lane = lax.broadcasted_iota(jnp.int32, (ROWS, HALF), 1)
 
     def place(w):
-        y, x = pos_ref[2 * w], pos_ref[2 * w + 1]
+        y, x = pos_ref[0, 0, w, 0, 0], pos_ref[0, 0, w, 0, 1]
         q = jnp.minimum(lax.div(x, HALF), 1)
         return y, q, x - q * HALF
 
@@ -269,14 +271,15 @@
         return jnp.concatenate([jnp.where(own, v[0], v[1]), jnp.where(own, v[1], v[2])], 1)
 
     def finish_gather(copies):
-        arrived(copies, G_FX)
-        start(copies, G_FWD)
         arrived(copies, G_FI)
         start(copies, G_INF)
         arrived(copies, G_VI)
         start(copies, G_INV)
         arrived(copies, G_VX, G_CROSS, G_CROSS2, G_DIRECT, G_IN, G_IN2, G_FWD, G_INF, G_INV)
 
+    for copies in (g0, g1):
+        arrived(copies, G_FX)
+        start(copies, G_FWD)
     finish_gather(g0)
 
     for w in range(2):
@@ -288,7 +291,7 @@
             x_ref[w, 1, rows, :] = pr * ti + pi * tr
 
         rows_loop(TILE, enter)
-    transform(x_ref, mid, b_ref, mats, T_A, True, True)
+    transform(x_ref, b_ref, mats, T_A, True, True)
 
     finish_gather(g1)
 
@@ -303,7 +306,7 @@
             x_ref[w, 1, rows, :] = br * ti + bi * tr
 
         rows_loop(TILE, leave)
-    transform(x_ref, mid, x_ref, mats, T_F, True, False)
+    transform(x_ref, x_ref, mats, T_F, True, False)
 
     for w in range(2):
         def residual(r, w=w):
@@ -314,7 +317,7 @@
             x_ref[w, 1, rows, :] = fi * keep
 
         rows_loop(TILE, residual)
-    transform(x_ref, mid, x_ref, mats, T_FI, False, True)
+    transform(x_ref, x_ref, mats, T_FI, False, True)
 
     def turned(w, part, r, v):
         _, _, s = place(w)
@@ -344,7 +347,8 @@
         cross_rows, inner_rows = at(3 * HALF * core), at(3 * HALF * (1 - core))
         f_blk, v_blk = 3 * (1 - c), 3 * c
         table = {
-            S_CROSS: (has_x, has_x, tot.at[:, pl.ds(1 - c, 3), cross_rows, :], r_x.at[s], (ix, j)),
+            S_CORNER: (has_x, has_x, tot.at[:, f_blk, cross_rows, :], r_c.at[s], (ix, j)),
+            S_CROSS: (has_x, has_x, tot.at[:, pl.ds(1, 2), cross_rows, :], r_x.at[s], (ix, j)),
             S_DIRECT: (has_d, has_d, tot.at[:, v_blk, cross_rows, :], r_d.at[s], (ix, jv)),
             S_IN: (always, always, tot.at[:, :, inner_rows, :], r_in.at[s], (i_in, j)),
             S_FX: (has_f, has_v, tot.at[:, f_blk, x_rows_p, :], r_f.at[s, :, x_rows, :], (i, jf)),
@@ -368,20 +372,19 @@
 
         rows_loop(HALF, chunk)
 
-    def add_cross(s):
+    def add_corner(s):
         tot = tots[s]
-        blks = pl.ds(c, 3)
 
         def chunk(r):
             rows = pl.ds(pl.multiple_of(MARGIN + HALF * core + r, ROWS), ROWS)
-            tot[:, blks, rows, :] = tot[:, blks, rows, :] + r_x[s, :, :, pl.ds(r, ROWS), :]
+            tot[:, 3 * c, rows, :] = tot[:, 3 * c, rows, :] + r_c[s, :, pl.ds(r, ROWS), :]
 
         @pl.when(has_x)
         def _():
             rows_loop(HALF, chunk)
 
     def send_early(s, copies):
-        start(copies, S_CROSS, S_IN, S_FX, S_DIRECT)
+        start(copies, S_CORNER, S_IN, S_FX, S_CROSS, S_DIRECT)
 
     def send_inner(s, copies):
         arrived(copies, S_IN)
@@ -389,32 +392,42 @@
         start(copies, S_FI, S_VI)
 
     def send_late(s, copies):
-        arrived(copies, S_CROSS)
-        add_cross(s)
+        arrived(copies, S_CORNER)
+        add_corner(s)
         start(copies, S_VX)
 
+    def own_part(s):
+        def chunk(r):
+            rows, rows_p = pl.ds(r, ROWS), pl.ds(MARGIN + r, ROWS)
+            for k in range(2):
+                cols = slice(HALF * k, HALF * (k + 1))
+                out_ref[s, :, rows, cols] = pads[s][:, 1 + k, rows_p, :] - STEP * tots[s][:, 1 + k, rows_p, :]
+
+        rows_loop(TILE, chunk)
+
+    def take(s, copies, key, cond, rows0, cols, part):
+        if key is not None:
+            arrived(copies, key)
+
+        def chunk(r):
+            rows = pl.ds(pl.multiple_of(rows0 + r, ROWS), ROWS)
+            out_ref[s, :, rows, cols] = out_ref[s, :, rows, cols] - STEP * part(r)
+
+        @pl.when(cond)
+        def _():
+            rows_loop(HALF, chunk)
+
     def finish(s, copies):
-        tot = tots[s]
-        arrived(copies, S_DIRECT, S_FX, S_FI, S_VX, S_VI)
-
-        def add(cond, count, first_row, blk, buf):
-            def chunk(r):
-                rows = pl.ds(pl.multiple_of(first_row + r, ROWS), ROWS)
-                tot[:, blk, rows, :] = tot[:, blk, rows, :] + buf[s, :, pl.ds(r, ROWS), :]
-
-            @pl.when(cond)
-            def _():
-                rows_loop(count, chunk)
-
-        add(has_d, HALF, MARGIN + HALF * core, 1 + c, r_d)
-        add(has_v, TILE, MARGIN, 1 + c, r_f)
-        add(has_f, TILE, MARGIN, 2 - c, r_v)
-
-        def chunk(r):
-            for k in range(2):
-                out_ref[s, :, pl.ds(r, ROWS), HALF * k : HALF * (k + 1)] = tot[:, 1 + k, pl.ds(MARGIN + r, ROWS), :]
-
-        rows_loop(TILE, chunk)
+        x0, in0 = HALF * core, HALF * (1 - core)
+        f_cols, v_cols = at(HALF * c), at(HALF * (1 - c))
+        west, east = slice(0, HALF), slice(HALF, TILE)
+        take(s, copies, S_DIRECT, has_d, x0, f_cols, lambda r: r_d[s, :, pl.ds(r, ROWS), :])
+        take(s, copies, S_CROSS, has_x, x0, west, lambda r: r_x[s, :, 0, pl.ds(r, ROWS), :])
+        take(s, copies, None, has_x, x0, east, lambda r: r_x[s, :, 1, pl.ds(r, ROWS), :])
+        take(s, copies, S_FX, has_v, x0, f_cols, lambda r: r_f[s, :, pl.ds(pl.multiple_of(x0 + r, ROWS), ROWS), :])
+        take(s, copies, S_FI, has_v, in0, f_cols, lambda r: r_f[s, :, pl.ds(pl.multiple_of(in0 + r, ROWS), ROWS), :])
+        take(s, copies, S_VI, has_f, in0, v_cols, lambda r: r_v[s, :, pl.ds(pl.multiple_of(in0 + r, ROWS), ROWS), :])
+        take(s, copies, S_VX, has_f, x0, v_cols, lambda r: r_v[s, :, pl.ds(pl.multiple_of(x0 + r, ROWS), ROWS), :])
 
     for w in range(2):
         def second(r, w=w):
@@ -439,7 +452,8 @@
 
         rows_loop(TILE, back)
     send_inner(1, s1)
-    transform(x_ref, mid, x_ref, mats, T_AC, True, True)
+    send_late(1, s1)
+    transform(x_ref, x_ref, mats, T_AC, True, True)
     for w in range(2):
         def first_slice(r, w=w):
             rows = pl.ds(r, ROWS)
@@ -453,8 +467,9 @@
     s0 = scatter(0)
     send_early(0, s0)
     send_inner(0, s0)
-    send_late(1, s1)
     send_late(0, s0)
+    own_part(1)
+    own_part(0)
     finish(1, s1)
     finish(0, s0)
     for copies in (g0, g1, s0, s1):
@@ -462,15 +477,15 @@
 
 
 def body(n_row, n_col, mats, perms, obj, probe, amplitude, positions):
-    any_space = pl.BlockSpec(memory_space=pl.ANY)
+    any_space = pl.BlockSpec(memory_space=pltpu.HBM)
     vmem = pl.BlockSpec(memory_space=pltpu.VMEM)
     smem = pl.BlockSpec(memory_space=pltpu.SMEM)
     f32 = jnp.float32
     wide = pltpu.VMEM((2, 4, WIDE, HALF), f32)
     field = pltpu.VMEM((2, 2, TILE, TILE), f32)
-    gradient = pl.pallas_call(
+    return pl.pallas_call(
         functools.partial(kernel, n_row, n_col),
-        out_shape=jax.ShapeDtypeStruct((2, 2, TILE, TILE), f32),
+        out_shape=pltpu.VMEM((2, 2, TILE, TILE), f32),
         in_specs=[smem] + [any_space] * 5,
         out_specs=vmem,
         scratch_shapes=[
@@ -482,24 +497,23 @@
             pltpu.VMEM(perms.shape, jnp.bfloat16),
             pltpu.VMEM((2, TILE, TILE), f32),
             field, field, field,
-            pltpu.VMEM((2, TILE, TILE), f32),
             pltpu.VMEM((2, 2, 4, HALF, HALF), f32),
-            pltpu.VMEM((2, 2, 3, HALF, HALF), f32),
+            pltpu.VMEM((2, 2, 2, HALF, HALF), f32),
+            pltpu.VMEM((2, 2, HALF, HALF), f32),
             pltpu.VMEM((2, 2, HALF, HALF), f32),
             pltpu.VMEM((2, 2, TILE, HALF), f32),
             pltpu.VMEM((2, 2, TILE, HALF), f32),
             pltpu.SemaphoreType.DMA((8,)),
             pltpu.SemaphoreType.DMA((2, 12)),
             pltpu.SemaphoreType.DMA((2, 12)),
-            pltpu.SemaphoreType.DMA((2, 7)),
-            pltpu.SemaphoreType.DMA((2, 7)),
+            pltpu.SemaphoreType.DMA((2, 8)),
+            pltpu.SemaphoreType.DMA((2, 8)),
         ],
         compiler_params=pltpu.CompilerParams(
-            collective_id=0, has_side_effects=True, vmem_limit_bytes=56 * 1024 * 1024
+            collective_id=0, has_side_effects=True, vmem_limit_bytes=54 * 1024 * 1024
         ),
         cost_estimate=pl.CostEstimate(flops=3 * 10**9, bytes_accessed=8 * 10**6, transcendentals=131072),
-    )(positions.reshape(4), obj, probe, amplitude.reshape(2, TILE, TILE), mats, perms)
-    return obj - STEP * gradient
+    )(positions, obj, probe, amplitude.reshape(2, TILE, TILE), mats, perms)
 
 
 def solution(mesh):

time: 111 us -> 101 us (0.910); the launches traced: 110 us -> 101 us
  Pallas kernels: 105 us -> 100 us
  other arithmetic: 3.67 us -> 0 us
    pallas_call x1, Pallas kernels: 105 us -> 100 us  [body(): pl.pallas_call(functools.partial(kernel, n_row, n_col), out_shape=pltpu.V...]
    sub x1 -> x0, other arithmetic: 2.33 us -> none  [body(): return obj - STEP * gradient]
    unnamed x1 -> x0, other arithmetic: 1.34 us -> none
where the time goes in v2:
time: 101 us
  Pallas kernels  100 us (99%)
    pallas_call x1, Pallas kernels, body(): pl.pallas_call(functools.partial(kernel, n_row, n_col), out_shape=pltpu.V...  100 us

profile of v2, /device:TPU:26, one launch (start us, length us, event | category | flops | bytes accessed | tf_op | source)
XLA Modules:
  0.0 101.4 jit_solution(381366410917992722)
XLA Ops:
  0.0 100.4 %shard_map.64 = f32[2,2,256,256]{3,2,1,0:T(8,128)S(1)} custom-call(s32[1,1,2,1,2]{4,3,2,1,0:T(1,128)} %pos_ref.1, f32[2,2,256,256]{3,2,1,0:T(8,128)} %obj_ref.1, f32[2,256,256]{2,1,0:T(8,128)} %probe_ref.1, f32[2,256,256]{2,1,0:T(8,128)} %bitcast.1, bf16[4,2,2,2,256,256]{5,4,3,2,1,0:T(8,128)(2,1)} %constant.4.clone.mats_ref, ...), custom_call_target="tpu_custom_call" | custom-call | flops 3000000000 | bytes 8000000 | tf_op jit(solution)/shard_map/pallas_call | solution.py:486
  100.4 1.0 copy.8

commit v3 on v2

--- a/solution.py
+++ b/solution.py
@@ -99,7 +99,7 @@
         dst[w, 1, HALF:, :] = zd[HALF:]
         return carry
 
-    lax.fori_loop(0, 2, one, 0)
+    lax.fori_loop(0, 2, one, 0, unroll=True)
 
 
 ROWS = 32
@@ -110,7 +110,7 @@
         fn(pl.multiple_of(k * ROWS, ROWS))
         return carry
 
-    lax.fori_loop(0, count // ROWS, step, 0)
+    lax.fori_loop(0, count // ROWS, step, 0, unroll=4)
 
 
 def kernel(
@@ -212,10 +212,11 @@
             when(sent, copy.wait_send)
 
     g0, g1 = gather(0), gather(1)
-    rest = (G_IN, G_IN2, G_CROSS, G_CROSS2, G_FI, G_VI, G_VX, G_DIRECT)
+    inner_first = (G_FI, G_VI, G_IN, G_IN2)
+    then = (G_CROSS, G_CROSS2, G_VX, G_DIRECT)
     start(g0, G_FX)
     start(g1, G_FX)
-    start(g0, *rest)
+    start(g0, *inner_first, *then)
 
     inner = pl.ds(MARGIN, TILE)
     locals_ = [
@@ -231,7 +232,7 @@
     for copy in locals_:
         copy.start()
 
-    start(g1, *rest)
+    start(g1, *inner_first)
 
     def clear(r):
         for w in range(2):
@@ -281,6 +282,7 @@
         arrived(copies, G_FX)
         start(copies, G_FWD)
     finish_gather(g0)
+    start(g1, *then)
 
     for w in range(2):
         def enter(r, w=w):
@@ -329,10 +331,11 @@
         gbuf[w, part, 2, rows, :] = jnp.where(own, b, a)
         gbuf[w, part, 3, rows, :] = jnp.where(own, 0.0, b)
 
-    def add_up(tot):
+    def add_up(tot, row0, count, blocks):
         def chunk(r):
+            r = pl.multiple_of(row0 + r, ROWS)
             for part in range(2):
-                for k in range(4):
+                for k in blocks:
                     total = None
                     for w in range(2):
                         y, block, _ = place(w)
@@ -340,7 +343,7 @@
                         total = v if total is None else total + v
                     tot[part, k, pl.ds(r, ROWS), :] = total
 
-        rows_loop(WIDE, chunk)
+        rows_loop(count, chunk)
 
     def scatter(s):
         tot = tots[s]
@@ -384,7 +387,14 @@
             rows_loop(HALF, chunk)
 
     def send_early(s, copies):
-        start(copies, S_CORNER, S_IN, S_FX, S_CROSS, S_DIRECT)
+        everywhere = range(4)
+        add_up(tots[s], 3 * HALF * core, HALF, everywhere)
+        start(copies, S_CORNER, S_CROSS, S_DIRECT)
+        add_up(tots[s], MARGIN, TILE, (0, 3))
+        start(copies, S_FX)
+        add_up(tots[s], 3 * HALF * (1 - core), HALF, everywhere)
+        start(copies, S_IN)
+        add_up(tots[s], MARGIN, TILE, (1, 2))
 
     def send_inner(s, copies):
         arrived(copies, S_IN)
@@ -438,7 +448,6 @@
             turned(w, 1, r, br * ci - bi * cr)
 
         rows_loop(TILE, second)
-    add_up(tot1)
     s1 = scatter(1)
     send_early(1, s1)
 
@@ -463,7 +472,6 @@
             turned(w, 1, r, pr * ci - pi * cr)
 
         rows_loop(TILE, first_slice)
-    add_up(tot0)
     s0 = scatter(0)
     send_early(0, s0)
     send_inner(0, s0)

time: 101 us -> 97.1 us (0.961)
  Pallas kernels: 100 us -> 96.1 us
    pallas_call x1, Pallas kernels: 100 us -> 96.1 us  [body(): pl.pallas_call(functools.partial(kernel, n_row, n_col), out_shape=pltpu.V...]
where the time goes in v3:
time: 97.1 us; the launch traced here: 97 us
  Pallas kernels  96.1 us (99%)
    pallas_call x1, Pallas kernels, body(): pl.pallas_call(functools.partial(kernel, n_row, n_col), out_shape=pltpu.V...  96.1 us

profile of v3, /device:TPU:26, one launch (start us, length us, event | category | flops | bytes accessed | tf_op | source)
XLA Modules:
  0.0 97.0 jit_solution(12550055035142030605)
XLA Ops:
  0.0 96.1 %shard_map.64 = f32[2,2,256,256]{3,2,1,0:T(8,128)S(1)} custom-call(s32[1,1,2,1,2]{4,3,2,1,0:T(1,128)} %pos_ref.1, f32[2,2,256,256]{3,2,1,0:T(8,128)} %obj_ref.1, f32[2,256,256]{2,1,0:T(8,128)} %probe_ref.1, f32[2,256,256]{2,1,0:T(8,128)} %bitcast.1, bf16[4,2,2,2,256,256]{5,4,3,2,1,0:T(8,128)(2,1)} %constant.4.clone.mats_ref, ...), custom_call_target="tpu_custom_call" | custom-call | flops 3000000000 | bytes 8000000 | tf_op jit(solution)/shard_map/pallas_call | solution.py:494
  96.1 1.0 %copy.8 = f32[2,2,256,256]{3,2,1,0:T(8,128)} copy(f32[2,2,256,256]{3,2,1,0:T(8,128)S(1)} %shard_map.64) | data formatting | bytes 2097152

commit v4 on v3

--- a/solution.py
+++ b/solution.py
@@ -110,16 +110,16 @@
         fn(pl.multiple_of(k * ROWS, ROWS))
         return carry
 
-    lax.fori_loop(0, count // ROWS, step, 0, unroll=4)
+    lax.fori_loop(0, count // ROWS, step, 0, unroll=8 if count == TILE else 4)
 
 
 def kernel(
     n_row, n_col,
-    pos_ref, obj_ref, probe_ref, amp_ref, mats_ref, perms_ref,
+    pos_any, obj_ref, probe_ref, amp_ref, mats_ref, perms_ref,
     out_ref,
     pad0, pad1, tot0, tot1, gbuf, probe, amp, mats, perms, amp_p, x_ref, b_ref, t_ref,
     r_in, r_x, r_c, r_d, r_f, r_v,
-    local_sem, g_send, g_recv, s_send, s_recv,
+    pos_ref, local_sem, g_send, g_recv, s_send, s_recv,
 ):
     i, j = lax.axis_index("row"), lax.axis_index("col")
     core = lax.rem(i, 2)
@@ -143,16 +143,6 @@
 
     x_rows, in_rows = at(HALF * core), at(HALF * (1 - core))
     x_rows_p, in_rows_p = at(MARGIN + HALF * core), at(MARGIN + HALF * (1 - core))
-
-    border = jnp.logical_not(jnp.logical_and(has_x, jnp.logical_and(has_v, has_f)))
-
-    @pl.when(border)
-    def _():
-        def zero(r):
-            for pad in pads:
-                pad[:, :, pl.ds(r, ROWS), :] = jnp.zeros((2, 4, ROWS, HALF), jnp.float32)
-
-        rows_loop(WIDE, zero)
 
     barrier = pltpu.get_barrier_semaphore()
 
@@ -224,6 +214,7 @@
         for s, pad in enumerate(pads)
         for k in range(2)
     ] + [
+        pltpu.make_async_copy(pos_any, pos_ref, local_sem.at[8]),
         pltpu.make_async_copy(probe_ref, probe, local_sem.at[0]),
         pltpu.make_async_copy(amp_ref, amp, local_sem.at[1]),
         pltpu.make_async_copy(mats_ref, mats, local_sem.at[2]),
@@ -234,12 +225,27 @@
 
     start(g1, *inner_first)
 
+    def zero(cond, row0, count, blocks):
+        def chunk(r):
+            for pad in pads:
+                for k in blocks:
+                    pad[:, k, pl.ds(pl.multiple_of(row0 + r, ROWS), ROWS), :] = jnp.zeros((2, ROWS, HALF), jnp.float32)
+
+        @pl.when(jnp.logical_not(cond))
+        def _():
+            rows_loop(count, chunk)
+
+    zero(has_v, MARGIN, TILE, (3 * c,))
+    zero(has_f, MARGIN, TILE, (3 * (1 - c),))
+    zero(has_d, 3 * HALF * core, HALF, (3 * c,))
+    zero(has_x, 3 * HALF * core, HALF, (1, 2, 3 * (1 - c)))
+
     def clear(r):
         for w in range(2):
             gbuf[w, :, :, pl.ds(r, ROWS), :] = jnp.zeros((2, 5, ROWS, HALF), jnp.float32)
 
     rows_loop(3 * TILE, clear)
-    for copy in locals_[5:]:
+    for copy in locals_[6:]:
         copy.wait()
 
     def order(w, carry):
@@ -254,7 +260,7 @@
         return carry
 
     lax.fori_loop(0, 2, order, 0)
-    for copy in locals_[:5]:
+    for copy in locals_[:6]:
         copy.wait()
 
     lane = lax.broadcasted_iota(jnp.int32, (ROWS, HALF), 1)
@@ -487,14 +493,13 @@
 def body(n_row, n_col, mats, perms, obj, probe, amplitude, positions):
     any_space = pl.BlockSpec(memory_space=pltpu.HBM)
     vmem = pl.BlockSpec(memory_space=pltpu.VMEM)
-    smem = pl.BlockSpec(memory_space=pltpu.SMEM)
     f32 = jnp.float32
     wide = pltpu.VMEM((2, 4, WIDE, HALF), f32)
     field = pltpu.VMEM((2, 2, TILE, TILE), f32)
     return pl.pallas_call(
         functools.partial(kernel, n_row, n_col),
         out_shape=pltpu.VMEM((2, 2, TILE, TILE), f32),
-        in_specs=[smem] + [any_space] * 5,
+        in_specs=[any_space] * 6,
         out_specs=vmem,
         scratch_shapes=[
             wide, wide, wide, wide,
@@ -511,7 +516,8 @@
             pltpu.VMEM((2, 2, HALF, HALF), f32),
             pltpu.VMEM((2, 2, TILE, HALF), f32),
             pltpu.VMEM((2, 2, TILE, HALF), f32),
-            pltpu.SemaphoreType.DMA((8,)),
+            pltpu.SMEM((1, 1, 2, 1, 2), jnp.int32),
+            pltpu.SemaphoreType.DMA((9,)),
             pltpu.SemaphoreType.DMA((2, 12)),
             pltpu.SemaphoreType.DMA((2, 12)),
             pltpu.SemaphoreType.DMA((2, 8)),

time: 97.1 us -> 95.1 us (0.979)
  Pallas kernels: 96.1 us -> 94 us
    pallas_call x1, Pallas kernels: 96.1 us -> 94 us  [body(): pl.pallas_call(functools.partial(kernel, n_row, n_col), out_shape=pltpu.V...]
where the time goes in v4:
time: 95.1 us; the launch traced here: 95 us
  Pallas kernels  94 us (99%)
  local copies, waits for them, and re-layouts  0.97 us (1%)
    pallas_call x1, Pallas kernels, body(): pl.pallas_call(functools.partial(kernel, n_row, n_col), out_shape=pltpu.V...  94 us

profile of v4, /device:TPU:26, one launch (start us, length us, event | category | flops | bytes accessed | tf_op | source)
XLA Modules:
  0.0 95.0 jit_solution(7017272350356612804)
XLA Ops:
  0.0 94.0 %shard_map.64 = f32[2,2,256,256]{3,2,1,0:T(8,128)S(1)} custom-call(s32[1,1,2,1,2]{4,3,2,1,0:T(1,128)} %pos_any.1, f32[2,2,256,256]{3,2,1,0:T(8,128)} %obj_ref.1, f32[2,256,256]{2,1,0:T(8,128)} %probe_ref.1, f32[2,256,256]{2,1,0:T(8,128)} %bitcast.1, bf16[4,2,2,2,256,256]{5,4,3,2,1,0:T(8,128)(2,1)} %constant.4.clone.mats_ref, ...), custom_call_target="tpu_custom_call" | custom-call | flops 3000000000 | bytes 8000000 | tf_op jit(solution)/shard_map/pallas_call | solution.py:499
  94.0 1.0 %copy.8 = f32[2,2,256,256]{3,2,1,0:T(8,128)} copy(f32[2,2,256,256]{3,2,1,0:T(8,128)S(1)} %shard_map.64) | data formatting | bytes 2097152

commit v5 on v4

--- a/solution.py
+++ b/solution.py
@@ -395,7 +395,9 @@
     def send_early(s, copies):
         everywhere = range(4)
         add_up(tots[s], 3 * HALF * core, HALF, everywhere)
-        start(copies, S_CORNER, S_CROSS, S_DIRECT)
+        start(copies, S_CORNER, S_DIRECT)
+        if s == 1:
+            start(copies, S_CROSS)
         add_up(tots[s], MARGIN, TILE, (0, 3))
         start(copies, S_FX)
         add_up(tots[s], 3 * HALF * (1 - core), HALF, everywhere)
@@ -481,13 +483,16 @@
     s0 = scatter(0)
     send_early(0, s0)
     send_inner(0, s0)
+    left(s1, S_CROSS)
+    start(s0, S_CROSS)
     send_late(0, s0)
     own_part(1)
     own_part(0)
     finish(1, s1)
     finish(0, s0)
-    for copies in (g0, g1, s0, s1):
+    for copies in (g0, g1, s0):
         left(copies, *copies)
+    left(s1, *(k for k in s1 if k not in (S_CROSS,)))
 
 
 def body(n_row, n_col, mats, perms, obj, probe, amplitude, positions):

time: 95.1 us -> 94.2 us (level)
  the two profiles are of different devices: /device:TPU:26 before, /device:TPU:22 now
where the time goes in v5:
time: 94.2 us; the launch traced here: 94.1 us
  Pallas kernels  93.1 us (99%)
  local copies, waits for them, and re-layouts  0.97 us (1%)
    pallas_call x1, Pallas kernels, body(): pl.pallas_call(functools.partial(kernel, n_row, n_col), out_shape=pltpu.V...  93.1 us

profile of v5, /device:TPU:22, one launch (start us, length us, event | category | flops | bytes accessed | tf_op | source)
XLA Modules:
  0.0 94.1 jit_solution(4931502166378116276)
XLA Ops:
  0.0 93.1 %shard_map.64 = f32[2,2,256,256]{3,2,1,0:T(8,128)S(1)} custom-call(s32[1,1,2,1,2]{4,3,2,1,0:T(1,128)} %pos_any.1, f32[2,2,256,256]{3,2,1,0:T(8,128)} %obj_ref.1, f32[2,256,256]{2,1,0:T(8,128)} %probe_ref.1, f32[2,256,256]{2,1,0:T(8,128)} %bitcast.1, bf16[4,2,2,2,256,256]{5,4,3,2,1,0:T(8,128)(2,1)} %constant.4.clone.mats_ref, ...), custom_call_target="tpu_custom_call" | custom-call | flops 3000000000 | bytes 8000000 | tf_op jit(solution)/shard_map/pallas_call | solution.py:504
  93.1 1.0 %copy.8 = f32[2,2,256,256]{3,2,1,0:T(8,128)} copy(f32[2,2,256,256]{3,2,1,0:T(8,128)S(1)} %shard_map.64) | data formatting | bytes 2097152

commit v6 on v5

--- a/solution.py
+++ b/solution.py
@@ -75,13 +75,18 @@
 
 
 def transform(src, dst, mats, which, pre, post):
-    def one(w, carry):
+    sums, diffs = [], []
+    for w in range(2):
         xr, xi = src[w, 0], src[w, 1]
         r0, r1, i0, i1 = xr[:, :HALF], xr[:, HALF:], xi[:, :HALF], xi[:, HALF:]
         if pre:
             r0, r1, i0, i1 = r0 + r1, r0 - r1, i0 + i1, i0 - i1
-        ys = mm_right(jnp.concatenate([r0, i0], 1), mats[which, 0, 0, 0], mats[which, 0, 0, 1])
-        yd = mm_right(jnp.concatenate([r1, i1], 1), mats[which, 1, 0, 0], mats[which, 1, 0, 1])
+        sums.append(jnp.concatenate([r0, i0], 1))
+        diffs.append(jnp.concatenate([r1, i1], 1))
+    all_s = mm_right(jnp.concatenate(sums, 0), mats[which, 0, 0, 0], mats[which, 0, 0, 1])
+    all_d = mm_right(jnp.concatenate(diffs, 0), mats[which, 1, 0, 0], mats[which, 1, 0, 1])
+    for w in range(2):
+        ys, yd = all_s[TILE * w : TILE * (w + 1)], all_d[TILE * w : TILE * (w + 1)]
         if post:
             ys, yd = ys + yd, ys - yd
         yr = jnp.concatenate([ys[:, :HALF], yd[:, :HALF]], 1)
@@ -97,9 +102,6 @@
         dst[w, 0, HALF:, :] = zd[:HALF]
         dst[w, 1, :HALF, :] = zs[HALF:]
         dst[w, 1, HALF:, :] = zd[HALF:]
-        return carry
-
-    lax.fori_loop(0, 2, one, 0, unroll=True)
 
 
 ROWS = 32

time: 94.2 us -> 93.9 us (level)
  no operation moved by 1% of the time
where the time goes in v6:
time: 93.9 us; the launch traced here: 93.8 us
  Pallas kernels  92.8 us (99%)
  local copies, waits for them, and re-layouts  0.97 us (1%)
    pallas_call x1, Pallas kernels, body(): pl.pallas_call(functools.partial(kernel, n_row, n_col), out_shape=pltpu.V...  92.8 us

profile of v6, /device:TPU:22, one launch (start us, length us, event | category | flops | bytes accessed | tf_op | source)
XLA Modules:
  0.0 93.8 jit_solution(1801797049863766947)
XLA Ops:
  0.0 92.8 %shard_map.64 = f32[2,2,256,256]{3,2,1,0:T(8,128)S(1)} custom-call(s32[1,1,2,1,2]{4,3,2,1,0:T(1,128)} %pos_any.1, f32[2,2,256,256]{3,2,1,0:T(8,128)} %obj_ref.1, f32[2,256,256]{2,1,0:T(8,128)} %probe_ref.1, f32[2,256,256]{2,1,0:T(8,128)} %bitcast.1, bf16[4,2,2,2,256,256]{5,4,3,2,1,0:T(8,128)(2,1)} %constant.4.clone.mats_ref, ...), custom_call_target="tpu_custom_call" | custom-call | flops 3000000000 | bytes 8000000 | tf_op jit(solution)/shard_map/pallas_call | solution.py:506
  92.8 1.0 %copy.8 = f32[2,2,256,256]{3,2,1,0:T(8,128)} copy(f32[2,2,256,256]{3,2,1,0:T(8,128)S(1)} %shard_map.64) | data formatting | bytes 2097152

commit v7 on v6

--- a/solution.py
+++ b/solution.py
@@ -261,6 +261,9 @@
         amp_p[w] = total
         return carry
 
+    for copies in (g0, g1):
+        arrived(copies, G_FX)
+        start(copies, G_FWD)
     lax.fori_loop(0, 2, order, 0)
     for copy in locals_[:6]:
         copy.wait()
@@ -286,9 +289,6 @@
         start(copies, G_INV)
         arrived(copies, G_VX, G_CROSS, G_CROSS2, G_DIRECT, G_IN, G_IN2, G_FWD, G_INF, G_INV)
 
-    for copies in (g0, g1):
-        arrived(copies, G_FX)
-        start(copies, G_FWD)
     finish_gather(g0)
     start(g1, *then)
 

time: 93.9 us -> 93.9 us (level)
  no operation moved by 1% of the time
where the time goes in v7:
time: 93.9 us; the launch traced here: 93.8 us
  Pallas kernels  92.8 us (99%)
  local copies, waits for them, and re-layouts  0.97 us (1%)
    pallas_call x1, Pallas kernels, body(): pl.pallas_call(functools.partial(kernel, n_row, n_col), out_shape=pltpu.V...  92.8 us

profile of v7, /device:TPU:22, one launch (start us, length us, event | category | flops | bytes accessed | tf_op | source)
XLA Modules:
  0.0 93.8 jit_solution(1285401611801943053)
XLA Ops:
  0.0 92.8 %shard_map.64 = f32[2,2,256,256]{3,2,1,0:T(8,128)S(1)} custom-call(s32[1,1,2,1,2]{4,3,2,1,0:T(1,128)} %pos_any.1, f32[2,2,256,256]{3,2,1,0:T(8,128)} %obj_ref.1, f32[2,256,256]{2,1,0:T(8,128)} %probe_ref.1, f32[2,256,256]{2,1,0:T(8,128)} %bitcast.1, bf16[4,2,2,2,256,256]{5,4,3,2,1,0:T(8,128)(2,1)} %constant.4.clone.mats_ref, ...), custom_call_target="tpu_custom_call" | custom-call | flops 3000000000 | bytes 8000000 | tf_op jit(solution)/shard_map/pallas_call | solution.py:506
  92.8 1.0 %copy.8 = f32[2,2,256,256]{3,2,1,0:T(8,128)} copy(f32[2,2,256,256]{3,2,1,0:T(8,128)S(1)} %shard_map.64) | data formatting | bytes 2097152
